TPU v7x, 512 devices: a whole 4x4x16 slice. The times are simulated.
512 devices in a mesh: gx: 32 (over x, z_hi, y), gy: 16 (over z_lo, core).
Axes of the slice: x: 4, y: 4, z: 16 (z_hi: 2, z_lo: 8; z = z_hi * 8 + z_lo), core: 2. Of those that a mesh axis runs over, the one named last changes fastest.
Arguments:
- start_vectors: bfloat16 [128, 32, 128, 128], P('gx', 'gy'), may hold values from -6 to 6
- blocks: bfloat16 [128, 32, 7, 128, 128], P('gx', 'gy'), as said below
- neighbour: int32 [128, 32, 7], P('gx', 'gy'), may hold values from 0 to 8, as said below
- counts: int32 [128, 32], P('gx', 'gy'), may hold values from 1 to 7, as said below
Outputs:
- moments: float32 [5, 128], replicated
- last_vector: bfloat16 [128, 32, 128, 128], P('gx', 'gy')
Inputs may be any that keep to these rules, and one draw needn't show every extreme that they name: `neighbour`: each tile's 7 slots name the codes 0, 1, 3, 4, 5, 7, 8 once each, its live slots first; code 4 (the tile itself) is always live; tile t couples to tile t + d through a live slot exactly when tile t + d couples to t through a live slot of the opposite code. `counts`: one plus the number of the tile's live couplings to other tiles. The block of a live coupling of tile t + d back to tile t is the transpose of the block of tile t towards t + d; blocks of code 4 are symmetric.
All inputs are finite; a program needn't handle non-finite values.
Results may differ from a plain program's by a relative error of at most 0.0045.
Values may be sent and summed in bfloat16 or wider, within the bound.
A program may use at most 64 MiB of HBM per device.

v0:
```python
import jax
import jax.numpy as jnp
from jax import lax
from jax.sharding import PartitionSpec as P

ITERS = 4


def with_halo(cells, sides, width):
    for axis, dim in sides:
        count = lax.axis_size(axis)
        head = lax.slice_in_dim(cells, 0, width, axis=dim)
        tail = lax.slice_in_dim(cells, cells.shape[dim] - width, cells.shape[dim], axis=dim)
        cells = jnp.concatenate(
            [
                lax.ppermute(tail, axis, [(i, (i + 1) % count) for i in range(count)]),
                cells,
                lax.ppermute(head, axis, [((i + 1) % count, i) for i in range(count)]),
            ],
            axis=dim,
        )
    return cells


def local_apply(extended, blocks, neighbour, counts):
    tiles_x, tiles_y, slots = neighbour.shape
    vectors, orbitals = (extended.shape[2], extended.shape[3])
    flat = extended.reshape((tiles_x + 2) * (tiles_y + 2), vectors, orbitals)
    xs = jnp.arange(tiles_x, dtype=jnp.int32)[:, None] + 1
    ys = jnp.arange(tiles_y, dtype=jnp.int32)[None, :] + 1
    total = jnp.zeros((tiles_x, tiles_y, vectors, orbitals), jnp.float32)
    for slot in range(slots):
        code = neighbour[:, :, slot]
        index = (xs + code // 3 - 1) * (tiles_y + 2) + (ys + code % 3 - 1)
        piece = jnp.take(flat, index, axis=0)
        product = jnp.einsum(
            "xyrb,xyba->xyra", piece, blocks[:, :, slot], preferred_element_type=jnp.float32
        )
        live = (slot < counts).astype(jnp.float32)[:, :, None, None]
        total = total + live * product
    return total


def extend(vectors):
    along_x = with_halo(vectors, (("gx", 0),), 1)
    return with_halo(along_x, (("gy", 1),), 1)


def on_device(start_vectors, blocks, neighbour, counts):
    tiles_x, tiles_y = counts.shape
    total_rows = (
        tiles_x * lax.axis_size("gx") * tiles_y * lax.axis_size("gy") * start_vectors.shape[3]
    )
    first = start_vectors.astype(jnp.float32)
    partials = [jnp.sum(first * first, axis=(0, 1, 3))]
    previous = first
    current = local_apply(extend(start_vectors), blocks, neighbour, counts)
    partials.append(jnp.sum(first * current, axis=(0, 1, 3)))
    for step in range(ITERS - 1):
        image = local_apply(extend(current.astype(jnp.bfloat16)), blocks, neighbour, counts)
        following = 2.0 * image - previous
        previous, current = (current, following)
        partials.append(jnp.sum(first * current, axis=(0, 1, 3)))
    summed = jnp.stack([lax.psum(term, ("gx", "gy")) for term in partials])
    return (summed / total_rows, current.astype(jnp.bfloat16))


def solution(mesh):
    in_specs = (
        P("gx", "gy", None, None),
        P("gx", "gy", None, None, None),
        P("gx", "gy", None),
        P("gx", "gy"),
    )
    out_specs = (P(), P("gx", "gy", None, None))
    return jax.shard_map(
        on_device, mesh=mesh, in_specs=in_specs, out_specs=out_specs, check_vma=False
    )
```

profile of v0, /device:TPU:1, one launch (start us, length us, event | category | flops | bytes accessed | tf_op | source)
XLA Modules:
  0.0 365.0 jit_solution(12642964493823538940)
XLA Ops:
  1.5 4.0 %collective-permute-start = (bf16[1,2,128,128]{3,2,1,0:T(8,128)(2,1)S(1)}, bf16[1,2,128,128]{3,2,1,0:T(8,128)(2,1)S(1)}, u32[]{:S(2)}, u32[]{:S(2)}) collective-permute-start(bf16[1,2,128,128]{3,2,1,0:T(8,128)(2,1)S(1)} %get-tuple-element.49), channel_id=1, source_target_pairs={{0,16},{16,32},{32,48},{48,64},{64,80},{80,96},{96,112},{112,128},... | collective-permute-start | bytes 196616 | tf_op jit(solution)/shard_map/ppermute | solution.py:16
  5.6 18.8 %collective-permute-start.1 = (bf16[1,2,128,128]{3,2,1,0:T(8,128)(2,1)S(1)}, bf16[1,2,128,128]{3,2,1,0:T(8,128)(2,1)S(1)}, u32[]{:S(2)}, u32[]{:S(2)}) collective-permute-start(bf16[1,2,128,128]{3,2,1,0:T(8,128)(2,1)S(1)} %get-tuple-element.48), channel_id=1, source_target_pairs={{16,0},{32,16},{48,32},{64,48},{80,64},{96,80},{112,96},{128,112},... | collective-permute-start | bytes 196616 | tf_op jit(solution)/shard_map/ppermute | solution.py:18
  32.2 4.7 %collective-permute-start.3 = (bf16[6,1,128,128]{3,2,1,0:T(8,128)(2,1)S(1)}, bf16[6,1,128,128]{3,2,1,0:T(8,128)(2,1)S(1)}, u32[]{:S(2)}, u32[]{:S(2)}) collective-permute-start(bf16[6,1,128,128]{3,2,1,0:T(8,128)(2,1)S(1)} %get-tuple-element.41), channel_id=1, source_target_pairs={{1,0},{2,1},{3,2},{4,3},{5,4},{6,5},{7,6},{8,7},{9,8},{10,9},{11,1... | collective-permute-start | bytes 589832 | tf_op jit(solution)/shard_map/ppermute | solution.py:18
  36.9 1.9 collective-permute-start.2
  39.2 5.3 %collective-permute-done.2 = bf16[6,1,128,128]{3,2,1,0:T(8,128)(2,1)S(1)} collective-permute-done((bf16[6,1,128,128]{3,2,1,0:T(8,128)(2,1)S(1)}, bf16[6,1,128,128]{3,2,1,0:T(8,128)(2,1)S(1)}, u32[]{:S(2)}, u32[]{:S(2)}) %collective-permute-start.2) | collective-permute-done | bytes 196640 | tf_op jit(solution)/shard_map/ppermute | solution.py:16
  56.4 12.2 %collective-permute-start.5 = (bf16[1,2,128,128]{2,3,1,0:T(8,128)(2,1)S(1)}, bf16[1,2,128,128]{2,3,1,0:T(8,128)(2,1)S(1)}, u32[]{:S(2)}, u32[]{:S(2)}) collective-permute-start(bf16[1,2,128,128]{2,3,1,0:T(8,128)(2,1)S(1)} %get-tuple-element.47), channel_id=1, source_target_pairs={{16,0},{32,16},{48,32},{64,48},{80,64},{96,80},{112,96},{128,112},... | collective-permute-start | bytes 196616 | tf_op jit(solution)/shard_map/ppermute | solution.py:18
  68.6 1.9 collective-permute-start.4
  70.5 2.8 collective-permute-done.5
  73.3 13.4 %collective-permute-done.4 = bf16[1,2,128,128]{2,3,1,0:T(8,128)(2,1)S(1)} collective-permute-done((bf16[1,2,128,128]{2,3,1,0:T(8,128)(2,1)S(1)}, bf16[1,2,128,128]{2,3,1,0:T(8,128)(2,1)S(1)}, u32[]{:S(2)}, u32[]{:S(2)}) %collective-permute-start.4) | collective-permute-done | bytes 65568 | tf_op jit(solution)/shard_map/ppermute | solution.py:16
  87.4 12.2 %collective-permute-start.7 = (bf16[6,1,128,128]{2,3,1,0:T(8,128)(2,1)}, bf16[6,1,128,128]{2,3,1,0:T(8,128)(2,1)S(1)}, u32[]{:S(2)}, u32[]{:S(2)}) collective-permute-start(bf16[6,1,128,128]{2,3,1,0:T(8,128)(2,1)} %get-tuple-element.39), channel_id=1, source_target_pairs={{1,0},{2,1},{3,2},{4,3},{5,4},{6,5},{7,6},{8,7},{9,8},{10,9},{11,1... | collective-permute-start | bytes 589832 | tf_op jit(solution)/shard_map/ppermute | solution.py:18
  99.6 1.9 collective-permute-start.6
  131.5 1.9 collective-permute-start.9
  133.5 3.4 collective-permute-start.8
  136.9 14.6 %collective-permute-done.8 = bf16[1,2,128,128]{2,3,1,0:T(8,128)(2,1)S(1)} collective-permute-done((bf16[1,2,128,128]{2,3,1,0:T(8,128)(2,1)S(1)}, bf16[1,2,128,128]{2,3,1,0:T(8,128)(2,1)S(1)}, u32[]{:S(2)}, u32[]{:S(2)}) %collective-permute-start.8) | collective-permute-done | bytes 65568 | tf_op jit(solution)/shard_map/ppermute | solution.py:16
  151.6 11.8 %collective-permute-start.11 = (bf16[6,1,128,128]{2,3,1,0:T(8,128)(2,1)S(1)}, bf16[6,1,128,128]{2,3,1,0:T(8,128)(2,1)S(1)}, u32[]{:S(2)}, u32[]{:S(2)}) collective-permute-start(bf16[6,1,128,128]{2,3,1,0:T(8,128)(2,1)S(1)} %get-tuple-element.37), channel_id=1, source_target_pairs={{1,0},{2,1},{3,2},{4,3},{5,4},{6,5},{7,6},{8,7},{9,8},{10,9},{11,1... | collective-permute-start | bytes 589832 | tf_op jit(solution)/shard_map/ppermute | solution.py:18
  163.3 1.9 collective-permute-start.10
  165.3 2.9 collective-permute-done.10
  195.0 1.9 collective-permute-start.13
  196.9 3.4 collective-permute-start.12
  200.3 14.7 %collective-permute-done.12 = bf16[1,2,128,128]{2,3,1,0:T(8,128)(2,1)S(1)} collective-permute-done((bf16[1,2,128,128]{2,3,1,0:T(8,128)(2,1)S(1)}, bf16[1,2,128,128]{2,3,1,0:T(8,128)(2,1)S(1)}, u32[]{:S(2)}, u32[]{:S(2)}) %collective-permute-start.12) | collective-permute-done | bytes 65568 | tf_op jit(solution)/shard_map/ppermute | solution.py:16
  215.1 11.8 %collective-permute-start.15 = (bf16[6,1,128,128]{2,3,1,0:T(8,128)(2,1)S(1)}, bf16[6,1,128,128]{2,3,1,0:T(8,128)(2,1)S(1)}, u32[]{:S(2)}, u32[]{:S(2)}) collective-permute-start(bf16[6,1,128,128]{2,3,1,0:T(8,128)(2,1)S(1)} %get-tuple-element.35), channel_id=1, source_target_pairs={{1,0},{2,1},{3,2},{4,3},{5,4},{6,5},{7,6},{8,7},{9,8},{10,9},{11,1... | collective-permute-start | bytes 589832 | tf_op jit(solution)/shard_map/ppermute | solution.py:18
  226.9 2.1 collective-permute-start.14
  229.0 2.8 collective-permute-done.14
  258.1 105.4 %all-reduce = (f32[1,128]{1,0:T(1,128)S(1)}, f32[1,128]{1,0:T(1,128)S(1)}, f32[1,128]{1,0:T(1,128)S(1)}, f32[1,128]{1,0:T(1,128)S(1)}, f32[1,128]{1,0:T(1,128)S(1)}) all-reduce(f32[1,128]{1,0:T(1,128)S(1)} %bitcast.259, f32[1,128]{1,0:T(1,128)S(1)} %bitcast.256, ...), channel_id=1, replica_groups=mesh['gx'=32,'gy'=16] {'gx','gy'}, use_global_device_ids=true, to_apply=%region_1.2 | all-reduce | flops 640 | bytes 5120 | tf_op jit(solution)/shard_map/psum | solution.py:64
  (285 shorter events, 105.8 us)
Async XLA Ops:
  1.5 29.6 %collective-permute-start = (bf16[1,2,128,128]{3,2,1,0:T(8,128)(2,1)S(1)}, bf16[1,2,128,128]{3,2,1,0:T(8,128)(2,1)S(1)}, u32[]{:S(2)}, u32[]{:S(2)}) collective-permute-start(bf16[1,2,128,128]{3,2,1,0:T(8,128)(2,1)S(1)} %get-tuple-element.49), channel_id=1, source_target_pairs={{0,16},{16,32},{32,48},{48,64},{64,80},{80,96},{96,112},{112,128},... | collective-permute-start | bytes 196616 | tf_op jit(solution)/shard_map/ppermute | solution.py:16
  5.6 26.5 %collective-permute-start.1 = (bf16[1,2,128,128]{3,2,1,0:T(8,128)(2,1)S(1)}, bf16[1,2,128,128]{3,2,1,0:T(8,128)(2,1)S(1)}, u32[]{:S(2)}, u32[]{:S(2)}) collective-permute-start(bf16[1,2,128,128]{3,2,1,0:T(8,128)(2,1)S(1)} %get-tuple-element.48), channel_id=1, source_target_pairs={{16,0},{32,16},{48,32},{64,48},{80,64},{96,80},{112,96},{128,112},... | collective-permute-start | bytes 196616 | tf_op jit(solution)/shard_map/ppermute | solution.py:18
  28.4 27.2 %copy-start.50 = (pred[4,2]{1,0:T(4,128)(4,1)}, pred[4,2]{1,0:T(4,128)(4,1)S(1)}, u32[]{:S(2)}) copy-start(pred[4,2]{1,0:T(4,128)(4,1)S(1)} %get-tuple-element.21) | copy-start | bytes 28
  30.1 24.7 %copy-start.44 = (pred[4,2]{1,0:T(4,128)(4,1)}, pred[4,2]{1,0:T(4,128)(4,1)S(1)}, u32[]{:S(2)}) copy-start(pred[4,2]{1,0:T(4,128)(4,1)S(1)} %get-tuple-element.68) | copy-start | bytes 28
  30.1 25.1 %copy-start.42 = (pred[4,2]{1,0:T(4,128)(4,1)}, pred[4,2]{1,0:T(4,128)(4,1)S(1)}, u32[]{:S(2)}) copy-start(pred[4,2]{1,0:T(4,128)(4,1)S(1)} %get-tuple-element.70) | copy-start | bytes 28
  30.1 25.9 %copy-start.54 = (pred[4,2]{1,0:T(4,128)(4,1)}, pred[4,2]{1,0:T(4,128)(4,1)S(1)}, u32[]{:S(2)}) copy-start(pred[4,2]{1,0:T(4,128)(4,1)S(1)} %get-tuple-element.19) | copy-start | bytes 28
  30.9 25.0 %copy-start.26 = (f32[4,2]{1,0:T(4,128)}, f32[4,2]{1,0:T(4,128)S(1)}, u32[]{:S(2)}) copy-start(f32[4,2]{1,0:T(4,128)S(1)} %copy.253) | copy-start | bytes 100
  32.2 7.1 %collective-permute-start.3 = (bf16[6,1,128,128]{3,2,1,0:T(8,128)(2,1)S(1)}, bf16[6,1,128,128]{3,2,1,0:T(8,128)(2,1)S(1)}, u32[]{:S(2)}, u32[]{:S(2)}) collective-permute-start(bf16[6,1,128,128]{3,2,1,0:T(8,128)(2,1)S(1)} %get-tuple-element.41), channel_id=1, source_target_pairs={{1,0},{2,1},{3,2},{4,3},{5,4},{6,5},{7,6},{8,7},{9,8},{10,9},{11,1... | collective-permute-start | bytes 589832 | tf_op jit(solution)/shard_map/ppermute | solution.py:18
  36.9 7.6 %collective-permute-start.2 = (bf16[6,1,128,128]{3,2,1,0:T(8,128)(2,1)S(1)}, bf16[6,1,128,128]{3,2,1,0:T(8,128)(2,1)S(1)}, u32[]{:S(2)}, u32[]{:S(2)}) collective-permute-start(bf16[6,1,128,128]{3,2,1,0:T(8,128)(2,1)S(1)} %get-tuple-element.40), channel_id=1, source_target_pairs={{0,1},{1,2},{2,3},{3,4},{4,5},{5,6},{6,7},{7,8},{8,9},{9,10},{10,1... | collective-permute-start | bytes 589832 | tf_op jit(solution)/shard_map/ppermute | solution.py:16
  55.9 45.6 %copy-start.4 = (bf16[4,2,128,128]{3,2,1,0:T(8,128)(2,1)S(1)}, bf16[4,2,128,128]{3,2,1,0:T(8,128)(2,1)}, u32[]{:S(2)}) copy-start(bf16[4,2,128,128]{3,2,1,0:T(8,128)(2,1)} %param.6) | copy-start | bytes 786436
  56.4 16.9 %collective-permute-start.5 = (bf16[1,2,128,128]{2,3,1,0:T(8,128)(2,1)S(1)}, bf16[1,2,128,128]{2,3,1,0:T(8,128)(2,1)S(1)}, u32[]{:S(2)}, u32[]{:S(2)}) collective-permute-start(bf16[1,2,128,128]{2,3,1,0:T(8,128)(2,1)S(1)} %get-tuple-element.47), channel_id=1, source_target_pairs={{16,0},{32,16},{48,32},{64,48},{80,64},{96,80},{112,96},{128,112},... | collective-permute-start | bytes 196616 | tf_op jit(solution)/shard_map/ppermute | solution.py:18
  68.6 18.1 %collective-permute-start.4 = (bf16[1,2,128,128]{2,3,1,0:T(8,128)(2,1)S(1)}, bf16[1,2,128,128]{2,3,1,0:T(8,128)(2,1)S(1)}, u32[]{:S(2)}, u32[]{:S(2)}) collective-permute-start(bf16[1,2,128,128]{2,3,1,0:T(8,128)(2,1)S(1)} %get-tuple-element.46), channel_id=1, source_target_pairs={{0,16},{16,32},{32,48},{48,64},{64,80},{80,96},{96,112},{112,128},... | collective-permute-start | bytes 196616 | tf_op jit(solution)/shard_map/ppermute | solution.py:16
  87.4 15.0 %collective-permute-start.7 = (bf16[6,1,128,128]{2,3,1,0:T(8,128)(2,1)}, bf16[6,1,128,128]{2,3,1,0:T(8,128)(2,1)S(1)}, u32[]{:S(2)}, u32[]{:S(2)}) collective-permute-start(bf16[6,1,128,128]{2,3,1,0:T(8,128)(2,1)} %get-tuple-element.39), channel_id=1, source_target_pairs={{1,0},{2,1},{3,2},{4,3},{5,4},{6,5},{7,6},{8,7},{9,8},{10,9},{11,1... | collective-permute-start | bytes 589832 | tf_op jit(solution)/shard_map/ppermute | solution.py:18
  99.6 5.1 %collective-permute-start.6 = (bf16[6,1,128,128]{2,3,1,0:T(8,128)(2,1)S(1)}, bf16[6,1,128,128]{2,3,1,0:T(8,128)(2,1)}, u32[]{:S(2)}, u32[]{:S(2)}) collective-permute-start(bf16[6,1,128,128]{2,3,1,0:T(8,128)(2,1)S(1)} %get-tuple-element.38), channel_id=1, source_target_pairs={{0,1},{1,2},{2,3},{3,4},{4,5},{5,6},{6,7},{7,8},{8,9},{9,10},{10,1... | collective-permute-start | bytes 589832 | tf_op jit(solution)/shard_map/ppermute | solution.py:16
  131.5 36.8 %copy-start.41 = (s32[1024]{0:T(1024)S(1)}, s32[1024]{0:T(1024)}, u32[]{:S(2)}) copy-start(s32[1024]{0:T(1024)} %copy-done.40) | copy-start | bytes 12292
  131.5 5.3 %collective-permute-start.9 = (bf16[1,2,128,128]{2,3,1,0:T(8,128)(2,1)S(1)}, bf16[1,2,128,128]{2,3,1,0:T(8,128)(2,1)S(1)}, u32[]{:S(2)}, u32[]{:S(2)}) collective-permute-start(bf16[1,2,128,128]{2,3,1,0:T(8,128)(2,1)S(1)} %get-tuple-element.45), channel_id=1, source_target_pairs={{16,0},{32,16},{48,32},{64,48},{80,64},{96,80},{112,96},{128,112},... | collective-permute-start | bytes 196616 | tf_op jit(solution)/shard_map/ppermute | solution.py:18
  133.5 36.1 %copy-start.31 = (s32[1024]{0:T(1024)S(1)}, s32[1024]{0:T(1024)}, u32[]{:S(2)}) copy-start(s32[1024]{0:T(1024)} %copy-done.30) | copy-start | bytes 12292
  133.5 18.0 %collective-permute-start.8 = (bf16[1,2,128,128]{2,3,1,0:T(8,128)(2,1)S(1)}, bf16[1,2,128,128]{2,3,1,0:T(8,128)(2,1)S(1)}, u32[]{:S(2)}, u32[]{:S(2)}) collective-permute-start(bf16[1,2,128,128]{2,3,1,0:T(8,128)(2,1)S(1)} %get-tuple-element.44), channel_id=1, source_target_pairs={{0,16},{16,32},{32,48},{48,64},{64,80},{80,96},{96,112},{112,128},... | collective-permute-start | bytes 196616 | tf_op jit(solution)/shard_map/ppermute | solution.py:16
  151.6 13.7 %collective-permute-start.11 = (bf16[6,1,128,128]{2,3,1,0:T(8,128)(2,1)S(1)}, bf16[6,1,128,128]{2,3,1,0:T(8,128)(2,1)S(1)}, u32[]{:S(2)}, u32[]{:S(2)}) collective-permute-start(bf16[6,1,128,128]{2,3,1,0:T(8,128)(2,1)S(1)} %get-tuple-element.37), channel_id=1, source_target_pairs={{1,0},{2,1},{3,2},{4,3},{5,4},{6,5},{7,6},{8,7},{9,8},{10,9},{11,1... | collective-permute-start | bytes 589832 | tf_op jit(solution)/shard_map/ppermute | solution.py:18
  163.3 4.9 %collective-permute-start.10 = (bf16[6,1,128,128]{2,3,1,0:T(8,128)(2,1)S(1)}, bf16[6,1,128,128]{2,3,1,0:T(8,128)(2,1)S(1)}, u32[]{:S(2)}, u32[]{:S(2)}) collective-permute-start(bf16[6,1,128,128]{2,3,1,0:T(8,128)(2,1)S(1)} %get-tuple-element.36), channel_id=1, source_target_pairs={{0,1},{1,2},{2,3},{3,4},{4,5},{5,6},{6,7},{7,8},{8,9},{9,10},{10,1... | collective-permute-start | bytes 589832 | tf_op jit(solution)/shard_map/ppermute | solution.py:16
  195.0 5.3 %collective-permute-start.13 = (bf16[1,2,128,128]{2,3,1,0:T(8,128)(2,1)S(1)}, bf16[1,2,128,128]{2,3,1,0:T(8,128)(2,1)S(1)}, u32[]{:S(2)}, u32[]{:S(2)}) collective-permute-start(bf16[1,2,128,128]{2,3,1,0:T(8,128)(2,1)S(1)} %get-tuple-element.43), channel_id=1, source_target_pairs={{16,0},{32,16},{48,32},{64,48},{80,64},{96,80},{112,96},{128,112},... | collective-permute-start | bytes 196616 | tf_op jit(solution)/shard_map/ppermute | solution.py:18
  196.9 18.1 %collective-permute-start.12 = (bf16[1,2,128,128]{2,3,1,0:T(8,128)(2,1)S(1)}, bf16[1,2,128,128]{2,3,1,0:T(8,128)(2,1)S(1)}, u32[]{:S(2)}, u32[]{:S(2)}) collective-permute-start(bf16[1,2,128,128]{2,3,1,0:T(8,128)(2,1)S(1)} %get-tuple-element.42), channel_id=1, source_target_pairs={{0,16},{16,32},{32,48},{48,64},{64,80},{80,96},{96,112},{112,128},... | collective-permute-start | bytes 196616 | tf_op jit(solution)/shard_map/ppermute | solution.py:16
  215.1 13.9 %collective-permute-start.15 = (bf16[6,1,128,128]{2,3,1,0:T(8,128)(2,1)S(1)}, bf16[6,1,128,128]{2,3,1,0:T(8,128)(2,1)S(1)}, u32[]{:S(2)}, u32[]{:S(2)}) collective-permute-start(bf16[6,1,128,128]{2,3,1,0:T(8,128)(2,1)S(1)} %get-tuple-element.35), channel_id=1, source_target_pairs={{1,0},{2,1},{3,2},{4,3},{5,4},{6,5},{7,6},{8,7},{9,8},{10,9},{11,1... | collective-permute-start | bytes 589832 | tf_op jit(solution)/shard_map/ppermute | solution.py:18
  226.9 4.9 %collective-permute-start.14 = (bf16[6,1,128,128]{2,3,1,0:T(8,128)(2,1)S(1)}, bf16[6,1,128,128]{2,3,1,0:T(8,128)(2,1)S(1)}, u32[]{:S(2)}, u32[]{:S(2)}) collective-permute-start(bf16[6,1,128,128]{2,3,1,0:T(8,128)(2,1)S(1)} %get-tuple-element.34), channel_id=1, source_target_pairs={{0,1},{1,2},{2,3},{3,4},{4,5},{5,6},{6,7},{7,8},{8,9},{9,10},{10,1... | collective-permute-start | bytes 589832 | tf_op jit(solution)/shard_map/ppermute | solution.py:16
  (48 other events, 404.3 us)
where the time goes:
time: 367 us; the launch traced here: 365 us
  blocking collectives  105 us (29%)
  starting transfers between devices  95.8 us (26%)
  local copies, waits for them, and re-layouts  77.4 us (21%)
  waiting for transfers between devices  58.4 us (16%)
  matrix products  23.2 us (6%)
    psum x1, blocking collectives, on_device(): summed = jnp.stack([lax.psum(term, ('gx', 'gy')) for term in partials])  105 us
    ppermute x8, starting transfers between devices, with_halo(): lax.ppermute(head, axis, [((i + 1) % count, i) for i in range(count)])  75.3 us
    gather x49, local copies, waits for them, and re-layouts, local_apply(): piece = jnp.take(flat, index, axis=0)  65.7 us
    ppermute x8, waiting for transfers between devices, with_halo(): lax.ppermute(tail, axis, [(i, (i + 1) % count) for i in range(count)])  55.2 us
    dot_general x28, matrix products, local_apply(): jnp.einsum('xyrb,xyba->xyra', piece, blocks[:, :, slot], preferred_elemen...  23.2 us
    ppermute x8, starting transfers between devices, with_halo(): lax.ppermute(tail, axis, [(i, (i + 1) % count) for i in range(count)])  20.5 us
  transfers between devices with their start and end apart: 16, of which 9 were waited for; matrix products, arithmetic and copies ran while one was open for 2% of the time, Pallas kernels for 0%

commit v1 on v0

v1 whole, which is shorter than its diff:
```python
import functools

import jax
import jax.numpy as jnp
from jax import lax
from jax.experimental import pallas as pl
from jax.experimental.pallas import tpu as pltpu
from jax.sharding import PartitionSpec as P

ITERS = 4
GROUPS = 2
Y_SIZE = 4
Z_HALVES = 2
CORES = 2
MESH = pl.DeviceIdType.MESH


def kernel(
    gx_n, gy_n, groups, total_rows,
    start_ref, blocks_ref, code_ref, count_ref,
    moments_ref, last_ref,
    raw, wx, wy, b, v, acc, xh, yh, part, ga, gb, gc,
    load_sem, out_sem, send_sem, recv_sem, ga_sem, gb_send, gb_recv, gc_send, gc_recv,
):
    tiles_x, tiles_y, slots = code_ref.shape
    vectors, orb = start_ref.shape[2:]
    rows = vectors // groups
    pair = 2 * orb
    last = tiles_x - 1

    gx, gy = lax.axis_index("gx"), lax.axis_index("gy")
    east, west = lax.rem(gx + 1, gx_n), lax.rem(gx + gx_n - 1, gx_n)
    north, south = lax.rem(gy + 1, gy_n), lax.rem(gy + gy_n - 1, gy_n)

    x_size = gx_n // (Y_SIZE * Z_HALVES)
    z_lows = gy_n // CORES
    px = lax.div(gx, Y_SIZE * Z_HALVES)
    z_high = lax.rem(lax.div(gx, Y_SIZE), Z_HALVES)
    py = lax.rem(gx, Y_SIZE)
    z_low, core = lax.div(gy, CORES), lax.rem(gy, CORES)
    plane_n, line_n = x_size * Y_SIZE, Z_HALVES * z_lows
    my_plane, my_line = px * Y_SIZE + py, z_high * z_lows + z_low
    sibling = (gx, z_low * CORES + 1 - core)

    def plane_peer(p):
        peer_x, peer_y = lax.div(p, Y_SIZE), lax.rem(p, Y_SIZE)
        return (peer_x * (Y_SIZE * Z_HALVES) + z_high * Y_SIZE + peer_y, gy)

    def line_peer(p):
        high, low = lax.div(p, z_lows), lax.rem(p, z_lows)
        return (px * (Y_SIZE * Z_HALVES) + high * Y_SIZE + py, low * CORES + core)

    barrier = pltpu.get_barrier_semaphore()

    def greet(device):
        pl.semaphore_signal(barrier, inc=1, device_id=device, device_id_type=MESH)

    for device in (
        (east, gy), (west, gy), (east, north), (west, south), (gx, north), (gx, south), sibling,
    ):
        greet(device)

    @pl.loop(1, line_n)
    def _(j):
        greet(line_peer(lax.rem(my_line + j, line_n)))

    @pl.loop(1, plane_n)
    def _(j):
        greet(plane_peer(lax.rem(my_plane + j, plane_n)))

    load_start = pltpu.make_async_copy(start_ref, b.at[0], load_sem.at[0])
    load_blocks = pltpu.make_async_copy(
        blocks_ref, raw.at[:, :, pl.ds(0, slots)], load_sem.at[1]
    )
    load_blocks.start()
    load_start.start()

    def rows_of(g):
        return pl.ds(pl.multiple_of(g * rows, rows), rows)

    def messages(k, g):
        r = rows_of(g)
        ends = (
            (b.at[k, last, :, r], xh.at[k, 0, :, r], (east, gy)),
            (b.at[k, 0, :, r], xh.at[k, 1, :, r], (west, gy)),
            (b.at[k, last, 1, r], yh.at[k, 0, 0, r], (east, north)),
            (b.at[k, 0, 0, r], yh.at[k, 1, tiles_x, r], (west, south)),
            (b.at[k, :, 1, r], yh.at[k, 0, pl.ds(1, tiles_x), r], (gx, north)),
            (b.at[k, :, 0, r], yh.at[k, 1, pl.ds(0, tiles_x), r], (gx, south)),
        )
        return [
            pltpu.make_async_remote_copy(
                src_ref=source,
                dst_ref=target,
                send_sem=send_sem.at[k * groups + g, m],
                recv_sem=recv_sem.at[k * groups + g, m],
                device_id=device,
                device_id_type=MESH,
            )
            for m, (source, target, device) in enumerate(ends)
        ]

    def interior(k, g):
        r = rows_of(g)
        for x in range(tiles_x):
            low, high = max(x - 1, 0), min(x + 1, last)
            left = jnp.concatenate(
                [b[k, s, y, r, :] for s in range(low, high + 1) for y in range(2)], axis=1
            )
            right = wx[x, (low - x + 1) * pair : (high - x + 2) * pair, :]
            acc[g, x] = jnp.dot(left, right, preferred_element_type=jnp.float32)

    def rim(k, g, x, side):
        r = rows_of(g)
        left = jnp.concatenate([yh[k, side, x, r, :], yh[k, side, x + 1, r, :]], axis=1)
        return jnp.dot(left, wy[x, side], preferred_element_type=jnp.float32)

    def finish(k, g, x, image):
        r = rows_of(g)
        scale = jnp.where(k == 0, 1.0, 2.0)
        value = scale * image - v[k, x, r, :]
        v[k + 2, x, r, :] = value
        rounded = value.astype(jnp.bfloat16)
        for y in range(2):
            b[k + 1, x, y, r, :] = rounded[:, y * orb : (y + 1) * orb]

    load_start.wait()
    v[0] = jnp.zeros(v.shape[1:], v.dtype)
    for x in range(tiles_x):
        for y in range(2):
            v[1, x, :, y * orb : (y + 1) * orb] = b[0, x, y].astype(jnp.float32)
            raw[x, y, slots] = jnp.zeros((orb, orb), raw.dtype)
    load_blocks.wait()

    @pl.loop(0, tiles_x)
    def _(x):
        for t in range(2):
            codes = [code_ref[x, t, j] for j in range(slots)]
            live = count_ref[x, t]

            def block(code):
                slot = jnp.int32(0)
                for j in range(1, slots):
                    slot = jnp.where(codes[j] == code, j, slot)
                return raw[x, t, jnp.where(slot < live, slot, slots)]

            for shift in range(3):
                for s in range(2):
                    code = 3 * shift + s - t + 1
                    wx[
                        x,
                        shift * pair + s * orb : shift * pair + (s + 1) * orb,
                        t * orb : (t + 1) * orb,
                    ] = jnp.zeros((orb, orb), wx.dtype) if code in (2, 6) else block(code)
            for s, code in enumerate(((0, 3), (5, 8))[t]):
                wy[x, t, s * orb : (s + 1) * orb, :] = block(code)

    @pl.loop(0, groups)
    def _(g):
        interior(0, g)

    pl.semaphore_wait(barrier, 7 + line_n - 1 + plane_n - 1)

    @pl.loop(0, groups)
    def _(g):
        for copy in messages(0, g):
            copy.start()

    def to_sibling():
        return pltpu.make_async_remote_copy(
            src_ref=ga.at[core], dst_ref=ga.at[core], send_sem=ga_sem.at[0], recv_sem=ga_sem.at[1],
            device_id=sibling, device_id_type=MESH,
        )

    def to_plane(p, slot):
        return pltpu.make_async_remote_copy(
            src_ref=gb.at[slot], dst_ref=gb.at[slot],
            send_sem=gb_send.at[p], recv_sem=gb_recv.at[slot],
            device_id=plane_peer(p), device_id_type=MESH,
        )

    def to_line(p, slot):
        return pltpu.make_async_remote_copy(
            src_ref=gc.at[slot], dst_ref=gc.at[slot],
            send_sem=gc_send.at[p], recv_sem=gc_recv.at[slot],
            device_id=line_peer(p), device_id_type=MESH,
        )

    @pl.loop(0, ITERS * groups)
    def _(i):
        k, g = lax.div(i, groups), lax.rem(i, groups)
        r = rows_of(g)
        incoming = messages(k, g)
        incoming[4].wait_recv()
        incoming[5].wait_recv()
        for x in range(1, last):
            finish(k, g, x, acc[g, x] + jnp.concatenate([rim(k, g, x, 0), rim(k, g, x, 1)], axis=1))
        acc[g, 0, :, orb:] += rim(k, g, 0, 1)
        acc[g, last, :, :orb] += rim(k, g, last, 0)
        for m in range(4):
            incoming[m].wait_recv()
        acc[g, 0, :, :orb] += rim(k, g, 0, 0)
        acc[g, last, :, orb:] += rim(k, g, last, 1)
        for x, side, low in ((0, 0, 0), (last, 1, 2 * pair)):
            left = jnp.concatenate([xh[k, side, y, r, :] for y in range(2)], axis=1)
            image = acc[g, x] + jnp.dot(
                left, wx[x, low : low + pair, :], preferred_element_type=jnp.float32
            )
            finish(k, g, x, image)

        @pl.when(k < ITERS - 1)
        def _():
            for copy in messages(k + 1, g):
                copy.start()
            interior(k + 1, g)

        @pl.when(k == ITERS - 1)
        def _():
            pltpu.make_async_copy(
                b.at[ITERS, :, :, r], last_ref.at[:, :, r], out_sem.at[g]
            ).start()

        @pl.when(k == 1)
        def _():
            for s, (one, two) in enumerate(((1, 1), (1, 2), (1, 3), (2, 3), (3, 3))):
                product = sum(v[one, x, r, :] * v[two, x, r, :] for x in range(tiles_x))
                part[s, r, :] = product[:, :orb] + product[:, orb:]

        @pl.when(i == 2 * groups - 1)
        def _():
            ga[core] = jnp.zeros(ga.shape[1:], ga.dtype)
            for s in range(5):
                ga[core, s : s + 1, :] = jnp.sum(part[s].T, axis=0, keepdims=True)
            to_sibling().start()

        @pl.when(i == 2 * groups)
        def _():
            to_sibling().wait_recv()
            gb[my_plane] = ga[0] + ga[1]

            @pl.loop(1, plane_n)
            def _(j):
                to_plane(lax.rem(my_plane + j, plane_n), my_plane).start()

        @pl.when(i == 3 * groups - 1)
        def _():
            @pl.loop(1, plane_n)
            def _(j):
                p = lax.rem(my_plane + j, plane_n)
                to_plane(p, p).wait_recv()

            gc[my_line] = jnp.sum(gb[...], axis=0)

            @pl.loop(1, line_n)
            def _(j):
                to_line(lax.rem(my_line + j, line_n), my_line).start()

    @pl.loop(1, line_n)
    def _(j):
        p = lax.rem(my_line + j, line_n)
        to_line(p, p).wait_recv()

    sums = jnp.sum(gc[...], axis=0) / total_rows
    moments_ref[0:3, :] = sums[0:3]
    moments_ref[3:4, :] = 2.0 * sums[3:4] - sums[1:2]
    moments_ref[4:5, :] = 2.0 * sums[4:5] - sums[0:1]

    @pl.loop(0, ITERS * groups)
    def _(i):
        for copy in messages(lax.div(i, groups), lax.rem(i, groups)):
            copy.wait_send()

    to_sibling().wait_send()

    @pl.loop(1, plane_n)
    def _(j):
        to_plane(lax.rem(my_plane + j, plane_n), my_plane).wait_send()

    @pl.loop(1, line_n)
    def _(j):
        to_line(lax.rem(my_line + j, line_n), my_line).wait_send()

    for g in range(groups):
        r = pl.ds(g * rows, rows)
        pltpu.make_async_copy(b.at[ITERS, :, :, r], last_ref.at[:, :, r], out_sem.at[g]).wait()


def on_device(start_vectors, blocks, neighbour, counts):
    gx_n, gy_n = lax.axis_size("gx"), lax.axis_size("gy")
    tiles_x, tiles_y, vectors, orb = start_vectors.shape
    slots = neighbour.shape[2]
    groups, rows = GROUPS, vectors // GROUPS
    plane_n, line_n = gx_n // Z_HALVES, Z_HALVES * gy_n // CORES
    total_rows = tiles_x * gx_n * tiles_y * gy_n * orb
    assert tiles_y == 2 and tiles_x >= 3
    half, full = jnp.bfloat16, jnp.float32
    dma = pltpu.SemaphoreType.DMA
    return pl.pallas_call(
        functools.partial(kernel, gx_n, gy_n, groups, total_rows),
        out_shape=(
            jax.ShapeDtypeStruct((5, vectors), full),
            jax.ShapeDtypeStruct(start_vectors.shape, half),
        ),
        in_specs=[
            pl.BlockSpec(memory_space=pltpu.HBM),
            pl.BlockSpec(memory_space=pltpu.HBM),
            pl.BlockSpec(memory_space=pltpu.SMEM),
            pl.BlockSpec(memory_space=pltpu.SMEM),
        ],
        out_specs=(
            pl.BlockSpec(memory_space=pltpu.VMEM),
            pl.BlockSpec(memory_space=pltpu.HBM),
        ),
        scratch_shapes=[
            pltpu.VMEM((tiles_x, 2, slots + 1, orb, orb), half),
            pltpu.VMEM((tiles_x, 6 * orb, 2 * orb), half),
            pltpu.VMEM((tiles_x, 2, 2 * orb, orb), half),
            pltpu.VMEM((ITERS + 1, tiles_x, 2, vectors, orb), half),
            pltpu.VMEM((ITERS + 2, tiles_x, vectors, 2 * orb), full),
            pltpu.VMEM((groups, tiles_x, rows, 2 * orb), full),
            pltpu.VMEM((ITERS, 2, 2, vectors, orb), half),
            pltpu.VMEM((ITERS, 2, tiles_x + 1, vectors, orb), half),
            pltpu.VMEM((5, vectors, orb), full),
            pltpu.VMEM((2, 8, vectors), full),
            pltpu.VMEM((plane_n, 8, vectors), full),
            pltpu.VMEM((line_n, 8, vectors), full),
            dma((2,)),
            dma((groups,)),
            dma((ITERS * groups, 6)),
            dma((ITERS * groups, 6)),
            dma((2,)),
            dma((plane_n,)),
            dma((plane_n,)),
            dma((line_n,)),
            dma((line_n,)),
        ],
        compiler_params=pltpu.CompilerParams(
            collective_id=0, has_side_effects=True, vmem_limit_bytes=40 * 1024 * 1024
        ),
    )(start_vectors, blocks, neighbour, counts)


def solution(mesh):
    in_specs = (
        P("gx", "gy", None, None),
        P("gx", "gy", None, None, None),
        P("gx", "gy", None),
        P("gx", "gy"),
    )
    out_specs = (P(), P("gx", "gy", None, None))
    return jax.shard_map(
        on_device, mesh=mesh, in_specs=in_specs, out_specs=out_specs, check_vma=False
    )
```

time: 367 us -> 84.4 us (0.23)
  blocking collectives: 105 us -> 0 us
  starting transfers between devices: 95.8 us -> 0 us
  Pallas kernels: 0 us -> 78.3 us
  local copies, waits for them, and re-layouts: 77.4 us -> 5.2 us
  waiting for transfers between devices: 58.4 us -> 0 us
  matrix products: 23.2 us -> 0 us
    psum x1 -> x0, blocking collectives: 105 us -> none  [on_device(): summed = jnp.stack([lax.psum(term, ('gx', 'gy')) for term in partials])]
    ppermute x16 -> x0, starting transfers between devices: 95.8 us -> none  [the longest x8 75.3 us: with_halo(): lax.ppermute(head, axis, [((i + 1) % count, i) for i in range(count)])]
    pallas_call x0 -> x1, Pallas kernels: none -> 78.3 us  [on_device(): pl.pallas_call(functools.partial(kernel, gx_n, gy_n, groups, total_rows),...]
    gather x49 -> x0, local copies, waits for them, and re-layouts: 65.7 us -> none  [local_apply(): piece = jnp.take(flat, index, axis=0)]
    ppermute x16 -> x0, waiting for transfers between devices: 58.4 us -> none  [the longest x8 55.2 us: with_halo(): lax.ppermute(tail, axis, [(i, (i + 1) % count) for i in range(count)])]
    dot_general x28 -> x0, matrix products: 23.2 us -> none  [local_apply(): jnp.einsum('xyrb,xyba->xyra', piece, blocks[:, :, slot], preferred_elemen...]
  transfers between devices with their start and end apart: 16 -> 0, of which waited for: 9 -> 0; matrix products, arithmetic and copies ran while one was open for 2% -> 0% of each run, Pallas kernels for 0% -> 0%
where the time goes in v1:
time: 84.4 us; the launch traced here: 84.2 us
  Pallas kernels  78.3 us (93%)
  local copies, waits for them, and re-layouts  5.2 us (6%)
    pallas_call x1, Pallas kernels, on_device(): pl.pallas_call(functools.partial(kernel, gx_n, gy_n, groups, total_rows),...  78.3 us
    unnamed x9, local copies, waits for them, and re-layouts  5.2 us

profile of v1, /device:TPU:1, one launch (start us, length us, event | category | flops | bytes accessed | tf_op | source)
XLA Modules:
  0.0 84.2 jit_solution(6058527198459984827)
XLA Ops:
  0.6 0.8 copy.6.count_ref
  1.4 0.0 copy-start
  1.4 1.5 %copy-done = bf16[4,2,7,128,128]{4,3,2,1,0:T(8,128)(2,1)S(1)} copy-done((bf16[4,2,7,128,128]{4,3,2,1,0:T(8,128)(2,1)S(1)}, bf16[4,2,7,128,128]{4,3,2,1,0:T(8,128)(2,1)}, u32[]{:S(2)}) %copy-start) | copy-done | bytes 1835032
  2.9 0.0 copy-start.1
  2.9 0.9 %copy-done.1 = bf16[4,2,128,128]{3,2,1,0:T(8,128)(2,1)S(1)} copy-done((bf16[4,2,128,128]{3,2,1,0:T(8,128)(2,1)S(1)}, bf16[4,2,128,128]{3,2,1,0:T(8,128)(2,1)}, u32[]{:S(2)}) %copy-start.1) | copy-done | bytes 262168
  3.8 0.0 copy-start.2
  3.8 0.7 copy-done.2
  4.5 78.3 %shard_map.59 = (f32[5,128]{1,0:T(8,128)S(1)}, bf16[4,2,128,128]{3,2,1,0:T(8,128)(2,1)S(1)}) custom-call(bf16[4,2,128,128]{3,2,1,0:T(8,128)(2,1)S(1)} %copy-done.1, bf16[4,2,7,128,128]{4,3,2,1,0:T(8,128)(2,1)S(1)} %copy-done, s32[4,2,7]{2,1,0:T(2,128)S(1)} %copy-done.2, s32[4,2]{1,0:T(4,128)S(1)} %copy.6.count_ref), custom_call_target="tpu_custom_call" | custom-call | tf_op jit(solution)/shard_map/pallas_call | solution.py:298
  82.9 0.6 copy.9
  83.5 0.7 copy.10
Async XLA Ops:
  1.4 1.5 %copy-start = (bf16[4,2,7,128,128]{4,3,2,1,0:T(8,128)(2,1)S(1)}, bf16[4,2,7,128,128]{4,3,2,1,0:T(8,128)(2,1)}, u32[]{:S(2)}) copy-start(bf16[4,2,7,128,128]{4,3,2,1,0:T(8,128)(2,1)} %blocks_ref.1) | copy-start | bytes 5505028
  2.9 0.9 %copy-start.1 = (bf16[4,2,128,128]{3,2,1,0:T(8,128)(2,1)S(1)}, bf16[4,2,128,128]{3,2,1,0:T(8,128)(2,1)}, u32[]{:S(2)}) copy-start(bf16[4,2,128,128]{3,2,1,0:T(8,128)(2,1)} %start_ref.1) | copy-start | bytes 786436
  3.8 0.7 copy-start.2

commit v2 on v1

--- a/solution.py
+++ b/solution.py
@@ -8,7 +8,7 @@
 from jax.sharding import PartitionSpec as P
 
 ITERS = 4
-GROUPS = 2
+GROUPS = 1
 Y_SIZE = 4
 Z_HALVES = 2
 CORES = 2
@@ -19,8 +19,8 @@
     gx_n, gy_n, groups, total_rows,
     start_ref, blocks_ref, code_ref, count_ref,
     moments_ref, last_ref,
-    raw, wx, wy, b, v, acc, xh, yh, part, ga, gb, gc,
-    load_sem, out_sem, send_sem, recv_sem, ga_sem, gb_send, gb_recv, gc_send, gc_recv,
+    raw, wx, wy, wg, b, v, acc, xh, yh, ts, tg, part, ga, gb, gc,
+    load_sem, out_sem, send_sem, recv_sem, block_sem, ga_sem, gb_send, gb_recv, gc_send, gc_recv,
 ):
     tiles_x, tiles_y, slots = code_ref.shape
     vectors, orb = start_ref.shape[2:]
@@ -78,26 +78,99 @@
     def rows_of(g):
         return pl.ds(pl.multiple_of(g * rows, rows), rows)
 
-    def messages(k, g):
-        r = rows_of(g)
+    def messages(m, g, first=0, stop=12):
+        k, r = 2 * m, rows_of(g)
+
+        def along_y(level):
+            return (
+                (b.at[level, :, 1, r], yh.at[level, 0, pl.ds(1, tiles_x), r], (gx, north)),
+                (b.at[level, :, 0, r], yh.at[level, 1, pl.ds(0, tiles_x), r], (gx, south)),
+            )
+
         ends = (
             (b.at[k, last, :, r], xh.at[k, 0, :, r], (east, gy)),
             (b.at[k, 0, :, r], xh.at[k, 1, :, r], (west, gy)),
             (b.at[k, last, 1, r], yh.at[k, 0, 0, r], (east, north)),
             (b.at[k, 0, 0, r], yh.at[k, 1, tiles_x, r], (west, south)),
-            (b.at[k, :, 1, r], yh.at[k, 0, pl.ds(1, tiles_x), r], (gx, north)),
-            (b.at[k, :, 0, r], yh.at[k, 1, pl.ds(0, tiles_x), r], (gx, south)),
+            *along_y(k),
+            (ts.at[m, 1, :, r], tg.at[m, 0, pl.ds(1, 2), r], (east, gy)),
+            (ts.at[m, 0, :, r], tg.at[m, 1, pl.ds(0, 2), r], (west, gy)),
+            (ts.at[m, 1, 1, r], tg.at[m, 0, 0, r], (east, north)),
+            (ts.at[m, 0, 0, r], tg.at[m, 1, 2, r], (west, south)),
+            *along_y(k + 1),
         )
         return [
             pltpu.make_async_remote_copy(
                 src_ref=source,
                 dst_ref=target,
-                send_sem=send_sem.at[k * groups + g, m],
-                recv_sem=recv_sem.at[k * groups + g, m],
+                send_sem=send_sem.at[m * groups + g, n],
+                recv_sem=recv_sem.at[m * groups + g, n],
                 device_id=device,
                 device_id_type=MESH,
             )
-            for m, (source, target, device) in enumerate(ends)
+            for n, (source, target, device) in enumerate(ends)
+            if first <= n < stop
+        ]
+
+    def from_corner(m, g, n):
+        return messages(m, g, n, n + 1)[0]
+
+    def send(m, g, n):
+        for copy in messages(m, g, n, n + 2):
+            copy.start()
+        if n in (0, 6):
+            @pl.when(gy == gy_n - 1)
+            def _():
+                from_corner(m, g, n + 2).start()
+
+            @pl.when(gy == 0)
+            def _():
+                from_corner(m, g, n + 3).start()
+
+    def pass_on(m, g, n):
+        k, r = 2 * m, rows_of(g)
+        for copy in messages(m, g, n, n + 2):
+            copy.wait_recv()
+        if n == 0:
+            ends = (
+                (xh.at[k, 0, 1, r], yh.at[k, 0, 0, r], north, gy < gy_n - 1),
+                (xh.at[k, 1, 0, r], yh.at[k, 1, tiles_x, r], south, gy > 0),
+            )
+        else:
+            ends = (
+                (tg.at[m, 0, 2, r], tg.at[m, 0, 0, r], north, gy < gy_n - 1),
+                (tg.at[m, 1, 0, r], tg.at[m, 1, 2, r], south, gy > 0),
+            )
+        for side, (source, target, row, allowed) in enumerate(ends):
+            copy = pltpu.make_async_remote_copy(
+                src_ref=source,
+                dst_ref=target,
+                send_sem=send_sem.at[m * groups + g, n + 2 + side],
+                recv_sem=recv_sem.at[m * groups + g, n + 2 + side],
+                device_id=(gx, row),
+                device_id_type=MESH,
+            )
+            pl.when(allowed)(copy.start)
+
+    def wait_for(m, g, first, stop):
+        for copy in messages(m, g, first, stop):
+            copy.wait_recv()
+
+    def block_messages():
+        ends = (
+            (wg.at[:, 2, pl.ds(0, orb)], wg.at[:, 0, pl.ds(0, orb)], (gx, north)),
+            (wg.at[:, 0, pl.ds(orb, orb)], wg.at[:, 2, pl.ds(orb, orb)], (gx, south)),
+        )
+        return [
+            pltpu.make_async_remote_copy(
+                src_ref=source,
+                dst_ref=target,
+                send_sem=block_sem.at[0, n],
+                recv_sem=block_sem.at[1, n],
+                device_id=device,
+                device_id_type=MESH,
+            )
+            for n, (source, target, device) in enumerate(ends)
         ]
 
     def interior(k, g):
@@ -115,10 +188,49 @@
         left = jnp.concatenate([yh[k, side, x, r, :], yh[k, side, x + 1, r, :]], axis=1)
         return jnp.dot(left, wy[x, side], preferred_element_type=jnp.float32)
 
+    def scale(k):
+        return jnp.where(k == 0, 1.0, 2.0)
+
+    def corner(k, g, side):
+        tile, x, low = ((0, 0, 0), (tiles_x, last, orb))[side]
+        return jnp.dot(
+            yh[k, side, tile, rows_of(g), :], wy[x, side, low : low + orb, :],
+            preferred_element_type=jnp.float32,
+        )
+
+    def beside_corner(k, g, side):
+        tile, x, low = ((1, 0, orb), (last, last, 0))[side]
+        return jnp.dot(
+            yh[k, side, tile, rows_of(g), :], wy[x, side, low : low + orb, :],
+            preferred_element_type=jnp.float32,
+        )
+
+    def across(k, g, side):
+        x, low = ((0, 0), (last, 2 * pair))[side]
+        left = jnp.concatenate([xh[k, side, y, rows_of(g), :] for y in range(2)], axis=1)
+        return jnp.dot(left, wx[x, low : low + pair, :], preferred_element_type=jnp.float32)
+
+    def ghosts(m, g, corners):
+        k, r = 2 * m, rows_of(g)
+        for side, x in ((0, 0), (1, last)):
+            column = [yh[k, 0, x + 1, r, :], b[k, x, 0, r, :], b[k, x, 1, r, :], yh[k, 1, x, r, :]]
+            for q in range(3):
+                if (q == 2 * side) != corners:
+                    continue
+                own = jnp.dot(
+                    jnp.concatenate(column[q : q + 2], axis=1), wg[side, q],
+                    preferred_element_type=jnp.float32,
+                )
+                value = tg[m, side, q, r, :].astype(jnp.float32) + scale(k) * own
+                rounded = value.astype(jnp.bfloat16)
+                if q == 2 * side:
+                    yh[k + 1, side, side * tiles_x, r, :] = rounded
+                else:
+                    xh[k + 1, side, q - 1 + side, r, :] = rounded
+
     def finish(k, g, x, image):
         r = rows_of(g)
-        scale = jnp.where(k == 0, 1.0, 2.0)
-        value = scale * image - v[k, x, r, :]
+        value = scale(k) * image - v[k, x, r, :]
         v[k + 2, x, r, :] = value
         rounded = value.astype(jnp.bfloat16)
         for y in range(2):
@@ -136,7 +248,7 @@
     def _(x):
         for t in range(2):
             codes = [code_ref[x, t, j] for j in range(slots)]
-            live = count_ref[x, t]
+            live = count_ref[t, x]
 
             def block(code):
                 slot = jnp.int32(0)
@@ -155,6 +267,15 @@
             for s, code in enumerate(((0, 3), (5, 8))[t]):
                 wy[x, t, s * orb : (s + 1) * orb, :] = block(code)
 
+    for t in range(2):
+        row = slice(t * orb, (t + 1) * orb)
+        wg[1, t, orb:, :] = wx[last, 2 * pair + t * orb : 2 * pair + (t + 1) * orb, row].T
+        wg[0, t + 1, :orb, :] = wx[0, row, row].T
+    wg[1, 1, :orb, :] = wx[last, 2 * pair + orb : 2 * pair + 2 * orb, :orb].T
+    wg[1, 2, :orb, :] = wy[last, 1, orb:, :].T
+    wg[0, 0, orb:, :] = wy[0, 0, :orb, :].T
+    wg[0, 1, orb:, :] = wx[0, :orb, orb:].T
+
     @pl.loop(0, groups)
     def _(g):
         interior(0, g)
@@ -163,8 +284,11 @@
 
     @pl.loop(0, groups)
     def _(g):
-        for copy in messages(0, g):
-            copy.start()
+        send(0, g, 4)
+        send(0, g, 0)
+
+    for copy in block_messages():
+        copy.start()
 
     def to_sibling():
         return pltpu.make_async_remote_copy(
@@ -186,75 +310,107 @@
             device_id=line_peer(p), device_id_type=MESH,
         )
 
-    @pl.loop(0, ITERS * groups)
-    def _(i):
-        k, g = lax.div(i, groups), lax.rem(i, groups)
-        r = rows_of(g)
-        incoming = messages(k, g)
-        incoming[4].wait_recv()
-        incoming[5].wait_recv()
-        for x in range(1, last):
-            finish(k, g, x, acc[g, x] + jnp.concatenate([rim(k, g, x, 0), rim(k, g, x, 1)], axis=1))
-        acc[g, 0, :, orb:] += rim(k, g, 0, 1)
-        acc[g, last, :, :orb] += rim(k, g, last, 0)
-        for m in range(4):
-            incoming[m].wait_recv()
-        acc[g, 0, :, :orb] += rim(k, g, 0, 0)
-        acc[g, last, :, orb:] += rim(k, g, last, 1)
-        for x, side, low in ((0, 0, 0), (last, 1, 2 * pair)):
-            left = jnp.concatenate([xh[k, side, y, r, :] for y in range(2)], axis=1)
-            image = acc[g, x] + jnp.dot(
-                left, wx[x, low : low + pair, :], preferred_element_type=jnp.float32
-            )
-            finish(k, g, x, image)
-
-        @pl.when(k < ITERS - 1)
+    @pl.loop(0, ITERS // 2)
+    def _(m):
+        k = 2 * m
+
+        @pl.loop(0, groups)
+        def _(g):
+            r = rows_of(g)
+            wait_for(m, g, 4, 6)
+            acc[g, 0, :, :orb] += beside_corner(k, g, 0)
+            acc[g, 0, :, orb:] += rim(k, g, 0, 1)
+            acc[g, last, :, :orb] += rim(k, g, last, 0)
+            acc[g, last, :, orb:] += beside_corner(k, g, 1)
+            for side, x in ((1, last), (0, 0)):
+                value = (scale(k) * acc[g, x] - v[k, x, r, :]).astype(jnp.bfloat16)
+                for y in range(2):
+                    ts[m, side, y, r, :] = value[:, y * orb : (y + 1) * orb]
+            send(m, g, 6)
+            for x in range(1, last):
+                rims = jnp.concatenate([rim(k, g, x, 0), rim(k, g, x, 1)], axis=1)
+                finish(k, g, x, acc[g, x] + rims)
+
+        @pl.when(m == 1)
         def _():
-            for copy in messages(k + 1, g):
-                copy.start()
+            to_sibling().wait_recv()
+            gb[my_plane] = ga[0] + ga[1]
+
+            @pl.loop(1, plane_n)
+            def _(j):
+                to_plane(lax.rem(my_plane + j, plane_n), my_plane).start()
+
+        @pl.loop(0, groups)
+        def _(g):
+            pass_on(m, g, 0)
+            for side, x in ((1, last), (0, 0)):
+                acc[g, x] += across(k, g, side)
+            wait_for(m, g, 2, 4)
+            acc[g, 0, :, :orb] += corner(k, g, 0)
+            acc[g, last, :, orb:] += corner(k, g, 1)
+            finish(k, g, last, acc[g, last])
+            finish(k, g, 0, acc[g, 0])
+            send(m, g, 10)
             interior(k + 1, g)
 
-        @pl.when(k == ITERS - 1)
+        @pl.when(m == 0)
         def _():
-            pltpu.make_async_copy(
-                b.at[ITERS, :, :, r], last_ref.at[:, :, r], out_sem.at[g]
-            ).start()
-
-        @pl.when(k == 1)
+            for copy in block_messages():
+                copy.wait_recv()
+
+        @pl.when(m == 1)
         def _():
-            for s, (one, two) in enumerate(((1, 1), (1, 2), (1, 3), (2, 3), (3, 3))):
-                product = sum(v[one, x, r, :] * v[two, x, r, :] for x in range(tiles_x))
-                part[s, r, :] = product[:, :orb] + product[:, orb:]
-
-        @pl.when(i == 2 * groups - 1)
+            @pl.loop(1, plane_n)
+            def _(j):
+                p = lax.rem(my_plane + j, plane_n)
+                to_plane(p, p).wait_recv()
+
+            gc[my_line] = jnp.sum(gb[...], axis=0)
+
+            @pl.loop(1, line_n)
+            def _(j):
+                to_line(lax.rem(my_line + j, line_n), my_line).start()
+
+        @pl.loop(0, groups)
+        def _(g):
+            r = rows_of(g)
+            pass_on(m, g, 6)
+            ghosts(m, g, False)
+            wait_for(m, g, 8, 12)
+            ghosts(m, g, True)
+            for side, x in ((1, last), (0, 0)):
+                rims = jnp.concatenate([rim(k + 1, g, x, 0), rim(k + 1, g, x, 1)], axis=1)
+                finish(k + 1, g, x, acc[g, x] + rims + across(k + 1, g, side))
+
+            @pl.when(m == 0)
+            def _():
+                send(1, g, 0)
+
+            for x in range(1, last):
+                rims = jnp.concatenate([rim(k + 1, g, x, 0), rim(k + 1, g, x, 1)], axis=1)
+                finish(k + 1, g, x, acc[g, x] + rims)
+
+            @pl.when(m == 0)
+            def _():
+                send(1, g, 4)
+                interior(2, g)
+                for s, (one, two) in enumerate(((1, 1), (1, 2), (1, 3), (2, 3), (3, 3))):
+                    product = sum(v[one, x, r, :] * v[two, x, r, :] for x in range(tiles_x))
+                    part[s, r, :] = product[:, :orb] + product[:, orb:]
+
+            @pl.when(m == 1)
+            def _():
+                pltpu.make_async_copy(
+                    b.at[ITERS, :, :, r], last_ref.at[:, :, r], out_sem.at[g]
+                ).start()
+
+        @pl.when(m == 0)
         def _():
             ga[core] = jnp.zeros(ga.shape[1:], ga.dtype)
             for s in range(5):
                 ga[core, s : s + 1, :] = jnp.sum(part[s].T, axis=0, keepdims=True)
             to_sibling().start()
 
-        @pl.when(i == 2 * groups)
-        def _():
-            to_sibling().wait_recv()
-            gb[my_plane] = ga[0] + ga[1]
-
-            @pl.loop(1, plane_n)
-            def _(j):
-                to_plane(lax.rem(my_plane + j, plane_n), my_plane).start()
-
-        @pl.when(i == 3 * groups - 1)
-        def _():
-            @pl.loop(1, plane_n)
-            def _(j):
-                p = lax.rem(my_plane + j, plane_n)
-                to_plane(p, p).wait_recv()
-
-            gc[my_line] = jnp.sum(gb[...], axis=0)
-
-            @pl.loop(1, line_n)
-            def _(j):
-                to_line(lax.rem(my_line + j, line_n), my_line).start()
-
     @pl.loop(1, line_n)
     def _(j):
         p = lax.rem(my_line + j, line_n)
@@ -265,10 +421,13 @@
     moments_ref[3:4, :] = 2.0 * sums[3:4] - sums[1:2]
     moments_ref[4:5, :] = 2.0 * sums[4:5] - sums[0:1]
 
-    @pl.loop(0, ITERS * groups)
+    @pl.loop(0, ITERS // 2 * groups)
     def _(i):
         for copy in messages(lax.div(i, groups), lax.rem(i, groups)):
             copy.wait_send()
+
+    for copy in block_messages():
+        copy.wait_send()
 
     to_sibling().wait_send()
 
@@ -315,19 +474,23 @@
             pltpu.VMEM((tiles_x, 2, slots + 1, orb, orb), half),
             pltpu.VMEM((tiles_x, 6 * orb, 2 * orb), half),
             pltpu.VMEM((tiles_x, 2, 2 * orb, orb), half),
+            pltpu.VMEM((2, 3, 2 * orb, orb), half),
             pltpu.VMEM((ITERS + 1, tiles_x, 2, vectors, orb), half),
             pltpu.VMEM((ITERS + 2, tiles_x, vectors, 2 * orb), full),
             pltpu.VMEM((groups, tiles_x, rows, 2 * orb), full),
             pltpu.VMEM((ITERS, 2, 2, vectors, orb), half),
             pltpu.VMEM((ITERS, 2, tiles_x + 1, vectors, orb), half),
+            pltpu.VMEM((ITERS // 2, 2, 2, vectors, orb), half),
+            pltpu.VMEM((ITERS // 2, 2, 3, vectors, orb), half),
             pltpu.VMEM((5, vectors, orb), full),
             pltpu.VMEM((2, 8, vectors), full),
             pltpu.VMEM((plane_n, 8, vectors), full),
             pltpu.VMEM((line_n, 8, vectors), full),
             dma((2,)),
             dma((groups,)),
-            dma((ITERS * groups, 6)),
-            dma((ITERS * groups, 6)),
+            dma((ITERS // 2 * groups, 12)),
+            dma((ITERS // 2 * groups, 12)),
+            dma((2, 2)),
             dma((2,)),
             dma((plane_n,)),
             dma((plane_n,)),
@@ -335,9 +498,9 @@
             dma((line_n,)),
         ],
         compiler_params=pltpu.CompilerParams(
-            collective_id=0, has_side_effects=True, vmem_limit_bytes=40 * 1024 * 1024
+            collective_id=0, has_side_effects=True, vmem_limit_bytes=54784 * 1024
         ),
-    )(start_vectors, blocks, neighbour, counts)
+    )(start_vectors, blocks, neighbour, counts.T)
 
 
 def solution(mesh):

time: 84.4 us -> 77.3 us (0.916)
  Pallas kernels: 78.3 us -> 73 us
  local copies, waits for them, and re-layouts: 5.2 us -> 2.66 us
    pallas_call x1, Pallas kernels: 78.3 us -> 73 us  [on_device(): pl.pallas_call(functools.partial(kernel, gx_n, gy_n, groups, total_rows),...]
    unnamed x9 -> x6, local copies, waits for them, and re-layouts: 5.2 us -> 2.66 us
where the time goes in v2:
time: 77.3 us; the launch traced here: 76.3 us
  Pallas kernels  73 us (94%)
  local copies, waits for them, and re-layouts  2.66 us (3%)
    pallas_call x1, Pallas kernels, on_device(): pl.pallas_call(functools.partial(kernel, gx_n, gy_n, groups, total_rows),...  73 us
    unnamed x6, local copies, waits for them, and re-layouts  2.66 us

profile of v2, /device:TPU:1, one launch (start us, length us, event | category | flops | bytes accessed | tf_op | source)
XLA Modules:
  0.0 76.3 jit_solution(2331920906072869006)
XLA Ops:
  0.6 0.0 copy-start
  0.6 0.7 copy-done
  1.3 0.0 copy-start.1
  1.3 0.7 copy-done.1
  2.0 73.0 %shard_map.59 = (f32[5,128]{1,0:T(8,128)S(1)}, bf16[4,2,128,128]{3,2,1,0:T(8,128)(2,1)S(1)}) custom-call(bf16[4,2,128,128]{3,2,1,0:T(8,128)(2,1)} %start_ref.1, bf16[4,2,7,128,128]{4,3,2,1,0:T(8,128)(2,1)} %blocks_ref.1, s32[4,2,7]{2,1,0:T(2,128)S(1)} %copy-done, s32[2,4]{1,0:T(2,128)S(1)} %bitcast.1), custom_call_target="tpu_custom_call" | custom-call | tf_op jit(solution)/shard_map/pallas_call | solution.py:457
  75.0 0.6 copy.8
  75.6 0.7 copy.9
Async XLA Ops:
  0.6 0.7 copy-start
  1.3 0.7 copy-start.1

commit v3 on v2

--- a/solution.py
+++ b/solution.py
@@ -12,6 +12,7 @@
 Y_SIZE = 4
 Z_HALVES = 2
 CORES = 2
+FIRST = 0
 MESH = pl.DeviceIdType.MESH
 
 
@@ -19,7 +20,7 @@
     gx_n, gy_n, groups, total_rows,
     start_ref, blocks_ref, code_ref, count_ref,
     moments_ref, last_ref,
-    raw, wx, wy, wg, b, v, acc, xh, yh, ts, tg, part, ga, gb, gc,
+    raw, wx, wy, wg, b, v, acc, xh, yh, ts, tg, ga, gb, gc,
     load_sem, out_sem, send_sem, recv_sem, block_sem, ga_sem, gb_send, gb_recv, gc_send, gc_recv,
 ):
     tiles_x, tiles_y, slots = code_ref.shape
@@ -115,8 +116,25 @@
     def from_corner(m, g, n):
         return messages(m, g, n, n + 1)[0]
 
+    def halves(m, g, n):
+        k = 2 * m
+        out = []
+        for y in range(2):
+            ends = (
+                ((b.at[k, last, y], xh.at[k, 0, y], east, 0), (b.at[k, 0, y], xh.at[k, 1, y], west, 1))
+                if n == 0
+                else ((ts.at[m, 1, y], tg.at[m, 0, 1 + y], east, 0), (ts.at[m, 0, y], tg.at[m, 1, y], west, 1))
+            )
+            for source, target, column, side in ends:
+                out.append(pltpu.make_async_remote_copy(
+                    src_ref=source, dst_ref=target,
+                    send_sem=send_sem.at[m * groups + g, n + side],
+                    recv_sem=recv_sem.at[m * groups + g, n + side],
+                    device_id=(column, gy), device_id_type=MESH))
+        return out
+
     def send(m, g, n):
-        for copy in messages(m, g, n, n + 2):
+        for copy in (messages(m, g, n, n + 2) if n not in (0, 6) else halves(m, g, n)):
             copy.start()
         if n in (0, 6):
             @pl.when(gy == gy_n - 1)
@@ -173,9 +191,9 @@
             for n, (source, target, device) in enumerate(ends)
         ]
 
-    def interior(k, g):
+    def interior(k, g, columns):
         r = rows_of(g)
-        for x in range(tiles_x):
+        for x in columns:
             low, high = max(x - 1, 0), min(x + 1, last)
             left = jnp.concatenate(
                 [b[k, s, y, r, :] for s in range(low, high + 1) for y in range(2)], axis=1
@@ -276,9 +294,11 @@
     wg[0, 0, orb:, :] = wy[0, 0, :orb, :].T
     wg[0, 1, orb:, :] = wx[0, :orb, orb:].T
 
+    edges, inner = (0, last), range(1, last)
+
     @pl.loop(0, groups)
     def _(g):
-        interior(0, g)
+        interior(0, g, edges)
 
     pl.semaphore_wait(barrier, 7 + line_n - 1 + plane_n - 1)
 
@@ -305,10 +325,26 @@
 
     def to_line(p, slot):
         return pltpu.make_async_remote_copy(
-            src_ref=gc.at[slot], dst_ref=gc.at[slot],
+            src_ref=gc.at[slot, pl.ds(0, 5)], dst_ref=gc.at[slot, pl.ds(0, 5)],
             send_sem=gc_send.at[p], recv_sem=gc_recv.at[slot],
             device_id=line_peer(p), device_id_type=MESH,
         )
+
+    def add_rims(k, g):
+        acc[g, 0, :, :orb] += beside_corner(k, g, 0)
+        acc[g, 0, :, orb:] += rim(k, g, 0, 1)
+        acc[g, last, :, :orb] += rim(k, g, last, 0)
+        acc[g, last, :, orb:] += beside_corner(k, g, 1)
+
+    def add_corners(k, g):
+        acc[g, 0, :, :orb] += corner(k, g, 0)
+        acc[g, last, :, orb:] += corner(k, g, 1)
+
+    def middle(k, g):
+        interior(k, g, inner)
+        for x in inner:
+            rims = jnp.concatenate([rim(k, g, x, 0), rim(k, g, x, 1)], axis=1)
+            finish(k, g, x, acc[g, x] + rims)
 
     @pl.loop(0, ITERS // 2)
     def _(m):
@@ -318,21 +354,22 @@
         def _(g):
             r = rows_of(g)
             wait_for(m, g, 4, 6)
-            acc[g, 0, :, :orb] += beside_corner(k, g, 0)
-            acc[g, 0, :, orb:] += rim(k, g, 0, 1)
-            acc[g, last, :, :orb] += rim(k, g, last, 0)
-            acc[g, last, :, orb:] += beside_corner(k, g, 1)
+            add_rims(k, g)
             for side, x in ((1, last), (0, 0)):
                 value = (scale(k) * acc[g, x] - v[k, x, r, :]).astype(jnp.bfloat16)
                 for y in range(2):
                     ts[m, side, y, r, :] = value[:, y * orb : (y + 1) * orb]
             send(m, g, 6)
-            for x in range(1, last):
-                rims = jnp.concatenate([rim(k, g, x, 0), rim(k, g, x, 1)], axis=1)
-                finish(k, g, x, acc[g, x] + rims)
+            middle(k, g)
 
         @pl.when(m == 1)
         def _():
+            ga[core] = jnp.zeros(ga.shape[1:], ga.dtype)
+            for s, (one, two) in enumerate(((1, 1), (1, 2), (1, 3), (2, 3), (3, 3))):
+                product = sum(v[one, x] * v[two, x] for x in range(tiles_x))
+                product = product[:, :orb] + product[:, orb:]
+                ga[core, s : s + 1, :] = jnp.sum(product.T, axis=0, keepdims=True)
+            to_sibling().start()
             to_sibling().wait_recv()
             gb[my_plane] = ga[0] + ga[1]
 
@@ -346,12 +383,11 @@
             for side, x in ((1, last), (0, 0)):
                 acc[g, x] += across(k, g, side)
             wait_for(m, g, 2, 4)
-            acc[g, 0, :, :orb] += corner(k, g, 0)
-            acc[g, last, :, orb:] += corner(k, g, 1)
+            add_corners(k, g)
             finish(k, g, last, acc[g, last])
             finish(k, g, 0, acc[g, 0])
             send(m, g, 10)
-            interior(k + 1, g)
+            interior(k + 1, g, edges)
 
         @pl.when(m == 0)
         def _():
@@ -376,27 +412,26 @@
             r = rows_of(g)
             pass_on(m, g, 6)
             ghosts(m, g, False)
-            wait_for(m, g, 8, 12)
+            for side, x in ((1, last), (0, 0)):
+                acc[g, x] += across(k + 1, g, side)
+            wait_for(m, g, 10, 12)
+            add_rims(k + 1, g)
+            wait_for(m, g, 8, 10)
             ghosts(m, g, True)
-            for side, x in ((1, last), (0, 0)):
-                rims = jnp.concatenate([rim(k + 1, g, x, 0), rim(k + 1, g, x, 1)], axis=1)
-                finish(k + 1, g, x, acc[g, x] + rims + across(k + 1, g, side))
+            add_corners(k + 1, g)
+            finish(k + 1, g, last, acc[g, last])
+            finish(k + 1, g, 0, acc[g, 0])
 
             @pl.when(m == 0)
             def _():
                 send(1, g, 0)
 
-            for x in range(1, last):
-                rims = jnp.concatenate([rim(k + 1, g, x, 0), rim(k + 1, g, x, 1)], axis=1)
-                finish(k + 1, g, x, acc[g, x] + rims)
+            middle(k + 1, g)
 
             @pl.when(m == 0)
             def _():
                 send(1, g, 4)
-                interior(2, g)
-                for s, (one, two) in enumerate(((1, 1), (1, 2), (1, 3), (2, 3), (3, 3))):
-                    product = sum(v[one, x, r, :] * v[two, x, r, :] for x in range(tiles_x))
-                    part[s, r, :] = product[:, :orb] + product[:, orb:]
+                interior(2, g, edges)
 
             @pl.when(m == 1)
             def _():
@@ -404,19 +439,12 @@
                     b.at[ITERS, :, :, r], last_ref.at[:, :, r], out_sem.at[g]
                 ).start()
 
-        @pl.when(m == 0)
-        def _():
-            ga[core] = jnp.zeros(ga.shape[1:], ga.dtype)
-            for s in range(5):
-                ga[core, s : s + 1, :] = jnp.sum(part[s].T, axis=0, keepdims=True)
-            to_sibling().start()
-
     @pl.loop(1, line_n)
     def _(j):
         p = lax.rem(my_line + j, line_n)
         to_line(p, p).wait_recv()
 
-    sums = jnp.sum(gc[...], axis=0) / total_rows
+    sums = jnp.sum(gc[:, 0:5, :], axis=0) / total_rows
     moments_ref[0:3, :] = sums[0:3]
     moments_ref[3:4, :] = 2.0 * sums[3:4] - sums[1:2]
     moments_ref[4:5, :] = 2.0 * sums[4:5] - sums[0:1]
@@ -482,7 +510,6 @@
             pltpu.VMEM((ITERS, 2, tiles_x + 1, vectors, orb), half),
             pltpu.VMEM((ITERS // 2, 2, 2, vectors, orb), half),
             pltpu.VMEM((ITERS // 2, 2, 3, vectors, orb), half),
-            pltpu.VMEM((5, vectors, orb), full),
             pltpu.VMEM((2, 8, vectors), full),
             pltpu.VMEM((plane_n, 8, vectors), full),
             pltpu.VMEM((line_n, 8, vectors), full),

time: 77.3 us -> 76.8 us (level)
  no operation moved by 1% of the time
where the time goes in v3:
time: 76.8 us; the launch traced here: 76.4 us
  Pallas kernels  73.1 us (95%)
  local copies, waits for them, and re-layouts  2.66 us (3%)
    pallas_call x1, Pallas kernels, on_device(): pl.pallas_call(functools.partial(kernel, gx_n, gy_n, groups, total_rows),...  73.1 us
    unnamed x6, local copies, waits for them, and re-layouts  2.66 us

profile of v3, /device:TPU:1, one launch (start us, length us, event | category | flops | bytes accessed | tf_op | source)
XLA Modules:
  0.0 76.4 jit_solution(7255044315999870788)
XLA Ops:
  0.6 0.0 copy-start
  0.6 0.7 copy-done
  1.3 0.0 copy-start.1
  1.3 0.7 copy-done.1
  2.0 73.1 %shard_map.59 = (f32[5,128]{1,0:T(8,128)S(1)}, bf16[4,2,128,128]{3,2,1,0:T(8,128)(2,1)S(1)}) custom-call(bf16[4,2,128,128]{3,2,1,0:T(8,128)(2,1)} %start_ref.1, bf16[4,2,7,128,128]{4,3,2,1,0:T(8,128)(2,1)} %blocks_ref.1, s32[4,2,7]{2,1,0:T(2,128)S(1)} %copy-done, s32[2,4]{1,0:T(2,128)S(1)} %bitcast.1), custom_call_target="tpu_custom_call" | custom-call | tf_op jit(solution)/shard_map/pallas_call | solution.py:485
  75.1 0.6 copy.8
  75.7 0.7 copy.9
Async XLA Ops:
  0.6 0.7 copy-start
  1.3 0.7 copy-start.1
